TPU v7x, 512 devices: a whole 4x8x8 slice. The times are simulated.
512 devices in a mesh: mp: 32 (over z, x), ctx: 16 (over y, core).
Axes of the slice: x: 4, y: 8, z: 8, core: 2. Of those that a mesh axis runs over, the one named last changes fastest.
Arguments:
- hidden_act: bfloat16 [16384, 25600], P('ctx', 'mp'), may hold values from -6 to 6
- out_grad: bfloat16 [16384, 5120], P('ctx', 'mp'), may hold values from -6 to 6
- proj_in: bfloat16 [25600, 64], P('mp'), may hold values from -0.0390625 to 0.0390625
- proj_out: bfloat16 [5120, 64], P('mp'), may hold values from -0.078125 to 0.078125
- queries: bfloat16 [8192, 4096], P('mp'), may hold values from -0.09375 to 0.09375
- lengths: int32 [256], replicated, may hold values from 1 to 3072, 16384 in all
- doc_order: int32 [256], replicated, may hold values from 0 to 255, as said below
Outputs:
- scores: float32 [256, 8192], P('ctx', 'mp')
Inputs may be any that keep to these rules, and one draw needn't show every extreme that they name: The lengths sum to 16384; the largest is exactly 3072. `doc_order`: each document appears exactly once; document 0 stands in one of the rows 128 to 143.
All inputs are finite; a program needn't handle non-finite values.
Results may differ from a plain program's by a relative error of at most 0.03.
Values may be sent and summed in bfloat16 or wider, within the bound.
A program may use at most 64 MiB of HBM per device.

v0:
```python
import math

import jax
import jax.numpy as jnp
from jax import lax
from jax.sharding import PartitionSpec as P


def doc_sums(both, lengths, first, low_rank):
    rows = both.shape[0]
    block = math.gcd(rows, 256)
    turns = rows // block
    doc_count = lengths.shape[0]
    ends = jnp.cumsum(lengths)
    starts = ends - lengths

    def step(total, turn):
        offset = turn * block
        piece = lax.dynamic_slice_in_dim(both, offset, block, 0)
        position = first + offset + jnp.arange(block, dtype=jnp.int32)
        inside = (position[:, None] >= starts[None, :]) & (position[:, None] < ends[None, :])
        member = inside.astype(jnp.bfloat16)
        left = piece[:, :low_rank]
        right = piece[:, low_rank:]
        weighted = (member[:, :, None] * left[:, None, :]).reshape(block, doc_count * low_rank)
        added = lax.dot_general(
            weighted, right, (((0,), (0,)), ((), ())), preferred_element_type=jnp.float32
        )
        return (total + added, None)

    empty = jnp.zeros((doc_count * low_rank, low_rank), jnp.float32)
    total, unused = lax.scan(step, empty, jnp.arange(turns, dtype=jnp.int32))
    return total.reshape(doc_count, low_rank * low_rank)


def score_rows(grads, queries):
    upper = grads.astype(jnp.bfloat16)
    lower = (grads - upper.astype(jnp.float32)).astype(jnp.bfloat16)
    dims = (((1,), (1,)), ((), ()))
    first_part = lax.dot_general(upper, queries, dims, preferred_element_type=jnp.float32)
    second_part = lax.dot_general(lower, queries, dims, preferred_element_type=jnp.float32)
    return first_part + second_part


def local(hidden_act, out_grad, proj_in, proj_out, queries, lengths, doc_order):
    tok_rows = hidden_act.shape[0]
    low_rank = proj_in.shape[1]
    part_left = jnp.dot(hidden_act, proj_in, preferred_element_type=jnp.float32)
    part_right = jnp.dot(out_grad, proj_out, preferred_element_type=jnp.float32)
    stacked = jnp.concatenate([part_left, part_right], axis=1)
    base = lax.axis_index("ctx") * tok_rows
    summed = lax.psum(stacked.astype(jnp.bfloat16), "mp")
    doc_grad = doc_sums(summed, lengths, base, low_rank)
    doc_grad = doc_grad / jnp.sqrt(lengths.astype(jnp.float32))[:, None]
    ordered = jnp.take(doc_grad, doc_order, axis=0)
    owned = lax.psum_scatter(
        ordered.astype(jnp.bfloat16), "ctx", scatter_dimension=0, tiled=True
    ).astype(jnp.float32)
    result = score_rows(owned, queries)
    return result


def solution(mesh):
    return jax.shard_map(
        local,
        mesh=mesh,
        in_specs=(
            P("ctx", "mp"),
            P("ctx", "mp"),
            P("mp", None),
            P("mp", None),
            P("mp", None),
            P(),
            P(),
        ),
        out_specs=P("ctx", "mp"),
        check_vma=False,
    )
```

profile of v0, /device:TPU:1, one launch (start us, length us, event | category | flops | bytes accessed | tf_op | source)
XLA Modules:
  0.0 328.0 jit_solution(9790778036674074170)
XLA Ops:
  6.5 0.0 copy-start
  6.5 0.0 all-reduce.2.cloned.1.call-start
  6.5 1.3 convolution_convert_fusion
  7.9 1.9 convolution_convert_fusion.1
  9.8 0.7 pad_maximum_fusion
  10.5 0.0 all-reduce.2.cloned.1.call-update
  10.6 0.0 reduce-scatter.2.cloned.1.call-start
  10.6 0.7 compare_select_fusion
  11.3 0.7 compare_and_fusion
  12.0 0.7 convert_sqrt_fusion
  12.7 1.0 reduce-window.9
  13.6 0.1 slice.13
  13.8 0.1 slice_reduce_fusion
  13.9 0.8 fusion.1
  14.6 152.7 %all-reduce.2.cloned.1.call-done = bf16[1024,128]{0,1:T(8,128)(2,1)} async-done(((bf16[1024,128]{0,1:T(8,128)(2,1)}), bf16[1024,128]{0,1:T(8,128)(2,1)}) %all-reduce.2.cloned.1.call-update) | async-done | bytes 262160 | tf_op jit(solution)/shard_map/psum | solution.py:52
  167.4 59.8 %while.11 = (s32[]{:T(128)}, f32[16384,64]{0,1:T(8,128)}, s32[4]{0:T(128)S(1)}, s32[]{:T(128)}, s32[256]{0:T(256)S(1)}, /*index=5*/s32[256]{0:T(256)S(1)}, bf16[...) while((s32[]{:T(128)}, f32[16384,64]{0,1:T(8,128)}, ...), condition=%wide.region_4.5_spmd.clone, body=%wide.region_3.4_spmd.clone.sunk | while | flops 543424768 | bytes 25563360 | solution.py:32
  167.4 0.7 dynamic_slice.10
  168.7 0.8 constant_dynamic-slice_fusion.2
  169.5 0.1 and_convert_fusion.2
  169.7 3.8 %broadcast_multiply_fusion.2 = bf16[256,256,64]{0,2,1:T(8,128)(2,1)} fusion(bf16[256,64]{0,1:T(8,128)(2,1)S(1)} %constant_dynamic-slice_fusion.2, bf16[256,256]{0,1:T(8,128)(2,1)S(1)} %and_convert_fusion.2), kind=kLoop, calls=%fused_computation.2.clone.1 | loop fusion | flops 4194304 | bytes 8552448 | tf_op jit(solution)/shard_map/while/body/eval_jaxpr/mul | solution.py:25
  173.4 8.0 %convolution_add_fusion.3 = f32[16384,64]{0,1:T(8,128)} fusion(bf16[256,16384]{0,1:T(8,128)(2,1)} %bitcast.20, f32[16384,64]{0,1:T(8,128)} %get-tuple-element.146, pred[]{:T(512)S(6)} %compare.3, bf16[1024,128]{0,1:T(8,128)(2,1)} %get-tuple-element.163, s32[]{:T(128)S(6)} %select_n.20, s32[]{:T(128)S(6)} %add.71), kind=kOutput, calls=%fused_computation.1.clone.1 | convolution fusion | flops 538968064 | bytes 16809992 | tf_op jit(solution)/shard_map/while/body/eval_jaxpr/dot_general | solution.py:26
  181.4 0.7 dynamic_slice.10
  182.8 0.8 constant_dynamic-slice_fusion.2
  183.5 0.1 and_convert_fusion.2
  183.7 3.8 %broadcast_multiply_fusion.2 = bf16[256,256,64]{0,2,1:T(8,128)(2,1)} fusion(bf16[256,64]{0,1:T(8,128)(2,1)S(1)} %constant_dynamic-slice_fusion.2, bf16[256,256]{0,1:T(8,128)(2,1)S(1)} %and_convert_fusion.2), kind=kLoop, calls=%fused_computation.2.clone.1 | loop fusion | flops 4194304 | bytes 8552448 | tf_op jit(solution)/shard_map/while/body/eval_jaxpr/mul | solution.py:25
  187.5 9.2 %convolution_add_fusion.3 = f32[16384,64]{0,1:T(8,128)} fusion(bf16[256,16384]{0,1:T(8,128)(2,1)} %bitcast.20, f32[16384,64]{0,1:T(8,128)} %get-tuple-element.146, pred[]{:T(512)S(6)} %compare.3, bf16[1024,128]{0,1:T(8,128)(2,1)} %get-tuple-element.163, s32[]{:T(128)S(6)} %select_n.20, s32[]{:T(128)S(6)} %add.71), kind=kOutput, calls=%fused_computation.1.clone.1 | convolution fusion | flops 538968064 | bytes 16809992 | tf_op jit(solution)/shard_map/while/body/eval_jaxpr/dot_general | solution.py:26
  196.7 0.7 dynamic_slice.10
  198.0 0.8 constant_dynamic-slice_fusion.2
  198.8 0.1 and_convert_fusion.2
  198.9 3.8 %broadcast_multiply_fusion.2 = bf16[256,256,64]{0,2,1:T(8,128)(2,1)} fusion(bf16[256,64]{0,1:T(8,128)(2,1)S(1)} %constant_dynamic-slice_fusion.2, bf16[256,256]{0,1:T(8,128)(2,1)S(1)} %and_convert_fusion.2), kind=kLoop, calls=%fused_computation.2.clone.1 | loop fusion | flops 4194304 | bytes 8552448 | tf_op jit(solution)/shard_map/while/body/eval_jaxpr/mul | solution.py:25
  202.7 9.2 %convolution_add_fusion.3 = f32[16384,64]{0,1:T(8,128)} fusion(bf16[256,16384]{0,1:T(8,128)(2,1)} %bitcast.20, f32[16384,64]{0,1:T(8,128)} %get-tuple-element.146, pred[]{:T(512)S(6)} %compare.3, bf16[1024,128]{0,1:T(8,128)(2,1)} %get-tuple-element.163, s32[]{:T(128)S(6)} %select_n.20, s32[]{:T(128)S(6)} %add.71), kind=kOutput, calls=%fused_computation.1.clone.1 | convolution fusion | flops 538968064 | bytes 16809992 | tf_op jit(solution)/shard_map/while/body/eval_jaxpr/dot_general | solution.py:26
  211.9 0.7 dynamic_slice.10
  213.3 0.8 constant_dynamic-slice_fusion.2
  214.0 0.1 and_convert_fusion.2
  214.2 3.8 %broadcast_multiply_fusion.2 = bf16[256,256,64]{0,2,1:T(8,128)(2,1)} fusion(bf16[256,64]{0,1:T(8,128)(2,1)S(1)} %constant_dynamic-slice_fusion.2, bf16[256,256]{0,1:T(8,128)(2,1)S(1)} %and_convert_fusion.2), kind=kLoop, calls=%fused_computation.2.clone.1 | loop fusion | flops 4194304 | bytes 8552448 | tf_op jit(solution)/shard_map/while/body/eval_jaxpr/mul | solution.py:25
  217.9 9.2 %convolution_add_fusion.3 = f32[16384,64]{0,1:T(8,128)} fusion(bf16[256,16384]{0,1:T(8,128)(2,1)} %bitcast.20, f32[16384,64]{0,1:T(8,128)} %get-tuple-element.146, pred[]{:T(512)S(6)} %compare.3, bf16[1024,128]{0,1:T(8,128)(2,1)} %get-tuple-element.163, s32[]{:T(128)S(6)} %select_n.20, s32[]{:T(128)S(6)} %add.71), kind=kOutput, calls=%fused_computation.1.clone.1 | convolution fusion | flops 538968064 | bytes 16809992 | tf_op jit(solution)/shard_map/while/body/eval_jaxpr/dot_general | solution.py:26
  227.1 6.9 %copy.10 = f32[16384,64]{1,0:T(8,128)} copy(f32[16384,64]{0,1:T(8,128)} %get-tuple-element.42) | data formatting | bytes 8388608 | tf_op jit(solution)/shard_map/while | solution.py:32
  234.0 7.9 %reshape.90 = f32[256,4096]{1,0:T(8,128)} reshape(f32[16384,64]{1,0:T(8,128)} %copy.10) | data formatting | bytes 8388608 | tf_op jit(solution)/shard_map/reshape | solution.py:33
  241.9 4.0 %broadcast_divide_fusion = bf16[256,4096]{1,0:T(8,128)(2,1)} fusion(f32[256,4096]{1,0:T(8,128)} %reshape.90, f32[256]{0:T(256)S(1)} %convert_sqrt_fusion), kind=kLoop, calls=%fused_computation.8 | loop fusion | flops 2097152 | bytes 6292480 | tf_op jit(solution)/shard_map/div | solution.py:54
  245.9 7.0 %gather_fusion = bf16[256,4096]{1,0:T(8,128)(2,1)} fusion(bf16[256,4096]{1,0:T(8,128)(2,1)} %broadcast_divide_fusion, s32[1024]{0:T(1024)S(1)} %pad_clamp_fusion), kind=kCustom, calls=%fused_computation | custom fusion | bytes 4195328 | tf_op jit(solution)/shard_map/jit(_take)/gather | solution.py:55
  253.0 3.5 %select_convert_fusion = bf16[256,4096]{1,0:T(8,128)(2,1)} fusion(bf16[256,4096]{1,0:T(8,128)(2,1)} %gather_fusion, pred[256]{0:T(512)(128)(4,1)S(1)} %compare_and_fusion), kind=kLoop, calls=%fused_computation.7 | loop fusion | flops 1048576 | bytes 4194560 | tf_op jit(solution)/shard_map/convert_element_type | solution.py:57
  256.4 0.0 reduce-scatter.2.cloned.1.call-update
  256.5 61.0 %reduce-scatter.2.cloned.1.call-done = bf16[16,4096]{1,0:T(8,128)(2,1)} async-done(((bf16[256,4096]{1,0:T(8,128)(2,1)}), bf16[16,4096]{1,0:T(8,128)(2,1)}) %reduce-scatter.2.cloned.1.call-update) | async-done | bytes 131088 | tf_op jit(solution)/shard_map/reduce_scatter | solution.py:56
  317.4 0.0 copy-done
  317.5 1.5 fusion.2
  319.0 2.2 convolution_add_fusion.1
  (8 shorter events, 0.1 us)
Async XLA Ops:
  6.5 310.9 %copy-start = (bf16[256,4096]{1,0:T(8,128)(2,1)S(1)}, bf16[256,4096]{1,0:T(8,128)(2,1)}, u32[]{:S(2)}) copy-start(bf16[256,4096]{1,0:T(8,128)(2,1)} %param.13) | copy-start | bytes 6291460
  6.5 160.8 %all-reduce.2.cloned.1.call-start = ((), (), s32[]{:S(2)}) async-start(), calls=%async_computation.1 | async-start | bytes 524288 | tf_op jit(solution)/shard_map/psum | solution.py:52
  10.6 306.9 %reduce-scatter.2.cloned.1.call-start = ((), (), s32[]{:S(2)}) async-start(), calls=%async_computation.2 | async-start | bytes 2228224 | tf_op jit(solution)/shard_map/reduce_scatter | solution.py:56
Sparse Core Ops, SparseCore 0:
  10.8 156.5 all-reduce.1
  256.6 60.8 reduce-scatter.1
where the time goes:
time: 330 us; the launch traced here: 328 us
  waiting for transfers between devices  214 us (65%)
  matrix products  42.6 us (13%)
  local copies, waits for them, and re-layouts  27.7 us (8%)
  other arithmetic  27.6 us (8%)
  between operations  13.4 us (4%)
    psum x1, waiting for transfers between devices, local(): summed = lax.psum(stacked.astype(jnp.bfloat16), 'mp')  153 us
    reduce_scatter x1, waiting for transfers between devices, local(): lax.psum_scatter(ordered.astype(jnp.bfloat16), 'ctx', scatter_dimension=0...  61 us
    dot_general x4, matrix products, step(): lax.dot_general(weighted, right, (((0,), (0,)), ((), ())), preferred_elem...  35.6 us
    mul x4, other arithmetic, step(): member[:, :, None] * left[:, None, :]  15.1 us
    reshape x1, local copies, waits for them, and re-layouts, doc_sums(): return total.reshape(doc_count, low_rank * low_rank)  7.89 us
    gather x1, local copies, waits for them, and re-layouts, local(): ordered = jnp.take(doc_grad, doc_order, axis=0)  7.04 us
    while x1, local copies, waits for them, and re-layouts, doc_sums(): total, unused = lax.scan(step, empty, jnp.arange(turns, dtype=jnp.int32))  6.89 us
  transfers between devices with their start and end apart: 2, of which 2 were waited for; matrix products, arithmetic and copies ran while one was open for 1% of the time, Pallas kernels for 0%

commit v1 on v0

v1 whole, which is shorter than its diff:
```python
import functools

import jax
import jax.numpy as jnp
from jax import lax
from jax.experimental import pallas as pl
from jax.experimental.pallas import tpu as pltpu
from jax.sharding import PartitionSpec as P

MESH = pl.DeviceIdType.MESH
NZ, NX, NY = 8, 4, 8
NMP, NCTX = NZ * NX, NY * 2
RANK = 64
ZL, XR = RANK // NZ, RANK // NX
F32, BF16 = jnp.float32, jnp.bfloat16


def ring(n):
    return sorted(range(1, n), key=lambda s: (-min(s, n - s), s))


def hops(s, n):
    return min(s, n - s)


Z_OFF, X_OFF, Y_OFF = ring(NZ), ring(NX), ring(NY)
MP_OFF = sorted(
    ((dz, dx) for dz in range(NZ) for dx in range(NX) if dz or dx),
    key=lambda o: (-hops(o[0], NZ) - hops(o[1], NX), o),
)


def kernel(
    hid, grad, pin, pout, qry, lens, order, out,
    vhid, vgrad, vpin, vpout, vq, qp, member, scale,
    lsend, lrecv, l2send, l2recv, rsend, rrecv, r2send, r2recv, gsend, grecv, fsend, frecv,
    load_sem, send_sem, recv_sem,
):
    mp, ctx = lax.axis_index("mp"), lax.axis_index("ctx")
    z, x = mp // NX, lax.rem(mp, NX)
    y, core = ctx // 2, lax.rem(ctx, 2)
    tok = vhid.shape[0]
    half = tok // 2
    quarter = tok // 4
    docs = member.shape[0]
    own = docs // NCTX

    def z_peer(s):
        return (lax.rem(z + s, NZ) * NX + x, ctx)

    def x_peer(s):
        return (z * NX + lax.rem(x + s, NX), ctx)

    def mp_peer(dz, dx):
        return (lax.rem(z + dz, NZ) * NX + lax.rem(x + dx, NX), ctx)

    def ctx_peers():
        for s in Y_OFF:
            for c in (0, 1):
                yield lax.rem(y + s, NY) * 2 + (core if c == 0 else 1 - core)
        yield y * 2 + 1 - core

    loads = [
        pltpu.make_async_copy(grad, vgrad, load_sem.at[0]),
        pltpu.make_async_copy(pout, vpout, load_sem.at[1]),
        pltpu.make_async_copy(pin, vpin, load_sem.at[2]),
        pltpu.make_async_copy(hid.at[pl.ds(0, half)], vhid.at[pl.ds(0, half)], load_sem.at[3]),
        pltpu.make_async_copy(hid.at[pl.ds(half, half)], vhid.at[pl.ds(half, half)], load_sem.at[4]),
        pltpu.make_async_copy(qry, vq, load_sem.at[5]),
    ]
    for load in loads:
        load.start()

    barrier = pltpu.get_barrier_semaphore()
    for dz, dx in MP_OFF:
        pl.semaphore_signal(barrier, inc=1, device_id=mp_peer(dz, dx), device_id_type=MESH)
    for peer in ctx_peers():
        pl.semaphore_signal(barrier, inc=1, device_id=(mp, peer), device_id_type=MESH)

    started = []

    def send(src, dst, phase, device):
        pltpu.make_async_remote_copy(
            src_ref=src, dst_ref=dst, send_sem=send_sem.at[phase], recv_sem=recv_sem.at[phase],
            device_id=device, device_id_type=MESH,
        ).start()

    def arrived(buf, count, phase):
        part = buf.at[pl.ds(0, count)]
        pltpu.make_async_copy(part, part, recv_sem.at[phase]).wait()
        started.append((part, phase))

    loads[0].wait()
    loads[1].wait()
    right = lax.dot_general(vpout[...], vgrad[...], (((0,), (1,)), ((), ())), preferred_element_type=F32)
    right = right.astype(BF16)
    for p in range(NX):
        rsend[p] = right[p * XR:(p + 1) * XR]
    pl.semaphore_wait(barrier, NMP - 1 + NCTX - 1)
    for s in X_OFF:
        send(rsend.at[lax.rem(x + s, NX)], rrecv.at[x], 0, x_peer(s))

    loads[2].wait()
    for b in range(2):
        loads[3 + b].wait()
        left = lax.dot_general(
            vpin[...], vhid[pl.ds(b * half, half), :], (((0,), (1,)), ((), ())), preferred_element_type=F32
        )
        for p in range(NZ):
            rows = left[p * ZL:(p + 1) * ZL]
            slot = jnp.concatenate([rows[:, :quarter], rows[:, quarter:]], axis=0)
            lsend[p, :, b * quarter:(b + 1) * quarter] = slot.astype(BF16)
    for s in Z_OFF:
        send(lsend.at[lax.rem(z + s, NZ)], lrecv.at[z], 1, z_peer(s))
    rrecv[x] = rsend[x]
    lrecv[z] = lsend[z]

    lane = lax.broadcasted_iota(jnp.int32, (docs, docs), 1)
    row = lax.broadcasted_iota(jnp.int32, (docs, docs), 0)
    length = lens[...].astype(F32)
    index = order[...].astype(F32)
    doc = jnp.sum(jnp.where(lane == row, index, 0.0), axis=1, keepdims=True)
    lane_f = lane.astype(F32)
    first = jnp.sum(jnp.where(lane_f < doc, length, 0.0), axis=1, keepdims=True)
    size = jnp.sum(jnp.where(lane_f == doc, length, 0.0), axis=1, keepdims=True)
    scale[...] = jnp.broadcast_to(1.0 / jnp.sqrt(size), scale.shape)
    place = (lax.broadcasted_iota(jnp.int32, (docs, tok), 1) + ctx * tok).astype(F32)
    member[...] = jnp.where((place >= first) & (place < first + size), 1.0, 0.0).astype(BF16)

    arrived(rrecv, NX - 1, 0)
    total = rrecv[0].astype(F32)
    for p in range(1, NX):
        total += rrecv[p].astype(F32)
    r2send[...] = total.astype(BF16)
    for s in Z_OFF:
        send(r2send, r2recv.at[z], 2, z_peer(s))
    r2recv[z] = r2send[...]

    arrived(lrecv, NZ - 1, 1)
    total = lrecv[0].astype(F32)
    for p in range(1, NZ):
        total += lrecv[p].astype(F32)
    l2send[...] = total.astype(BF16)
    for s in X_OFF:
        send(l2send, l2recv.at[x], 3, x_peer(s))
    l2recv[x] = l2send[...]

    loads[5].wait()
    wide = ZL * RANK
    cut = ZL * XR
    to = lax.broadcasted_iota(jnp.int32, (wide, wide), 1)
    at = lax.broadcasted_iota(jnp.int32, (wide, wide), 0)
    source = (to % cut) // XR * RANK + to // cut * XR + to % XR
    moved = jnp.where(at == source, 1.0, 0.0).astype(BF16)
    for p in range(NZ):
        piece = jnp.dot(vq[:, p * wide:(p + 1) * wide], moved, preferred_element_type=F32)
        qp[:, p * wide:(p + 1) * wide] = piece.astype(BF16)

    arrived(l2recv, NX - 1, 3)
    total = l2recv[0].astype(F32)
    for p in range(1, NX):
        total += l2recv[p].astype(F32)
    left = total.astype(BF16).astype(F32)
    arrived(r2recv, NZ - 1, 2)
    total = r2recv[0].astype(F32)
    for p in range(1, NZ):
        total += r2recv[p].astype(F32)
    right = total.astype(BF16).astype(F32)
    sums = jnp.zeros((docs, cut), F32)
    for b in range(2):
        for h in range(2):
            start = b * half + h * quarter
            piece = right[:, start:start + quarter]
            outer = jnp.concatenate(
                [left[h * ZL + i:h * ZL + i + 1, b * quarter:(b + 1) * quarter] * piece for i in range(ZL)], axis=0
            )
            sums += lax.dot_general(
                member[:, start:start + quarter], outer.astype(BF16), (((1,), (1,)), ((), ())),
                preferred_element_type=F32,
            )
    sums = sums.astype(BF16)
    for p in range(NCTX):
        gsend[p] = sums[p * own:(p + 1) * own]
    for peer in ctx_peers():
        send(gsend.at[peer], grecv.at[ctx], 4, (mp, peer))
    grecv[ctx] = gsend[ctx]

    arrived(grecv, NCTX - 1, 4)
    total = grecv[0].astype(F32)
    for p in range(1, NCTX):
        total += grecv[p].astype(F32)
    fsend[...] = (total * scale[pl.ds(ctx * own, own), :]).astype(BF16)
    for dz, dx in MP_OFF:
        send(fsend, frecv.at[mp], 5, mp_peer(dz, dx))
    frecv[mp] = fsend[...]
    arrived(frecv, NMP - 1, 5)

    grads = jnp.concatenate([frecv[p] for p in range(NMP)], axis=1)
    out[...] = lax.dot_general(grads, qp[...], (((1,), (1,)), ((), ())), preferred_element_type=F32)

    for part, phase in started:
        pltpu.make_async_copy(part, part, send_sem.at[phase]).wait()


def local(hidden_act, out_grad, proj_in, proj_out, queries, lengths, doc_order):
    tok, hid = hidden_act.shape
    feat = out_grad.shape[1]
    nq, wide = queries.shape
    docs = lengths.shape[0]
    own = docs // NCTX
    cut = ZL * XR
    anywhere = pl.BlockSpec(memory_space=pl.ANY)
    vmem = pl.BlockSpec(memory_space=pltpu.VMEM)
    scratch = [
        pltpu.VMEM((tok, hid), BF16),
        pltpu.VMEM((tok, feat), BF16),
        pltpu.VMEM((hid, RANK), BF16),
        pltpu.VMEM((feat, RANK), BF16),
        pltpu.VMEM((nq, wide), BF16),
        pltpu.VMEM((nq, wide), BF16),
        pltpu.VMEM((docs, tok), BF16),
        pltpu.VMEM((docs, cut), F32),
        pltpu.VMEM((NZ, 2 * ZL, tok // 2), BF16),
        pltpu.VMEM((NZ, 2 * ZL, tok // 2), BF16),
        pltpu.VMEM((2 * ZL, tok // 2), BF16),
        pltpu.VMEM((NX, 2 * ZL, tok // 2), BF16),
        pltpu.VMEM((NX, XR, tok), BF16),
        pltpu.VMEM((NX, XR, tok), BF16),
        pltpu.VMEM((XR, tok), BF16),
        pltpu.VMEM((NZ, XR, tok), BF16),
        pltpu.VMEM((NCTX, own, cut), BF16),
        pltpu.VMEM((NCTX, own, cut), BF16),
        pltpu.VMEM((own, cut), BF16),
        pltpu.VMEM((NMP, own, cut), BF16),
        pltpu.SemaphoreType.DMA((6,)),
        pltpu.SemaphoreType.DMA((6,)),
        pltpu.SemaphoreType.DMA((6,)),
    ]
    return pl.pallas_call(
        kernel,
        out_shape=jax.ShapeDtypeStruct((own, nq), F32),
        in_specs=[anywhere] * 5 + [vmem] * 2,
        out_specs=vmem,
        scratch_shapes=scratch,
        compiler_params=pltpu.CompilerParams(
            collective_id=0, has_side_effects=True, vmem_limit_bytes=40 * 1024 * 1024
        ),
    )(hidden_act, out_grad, proj_in, proj_out, queries, lengths.reshape(1, docs), doc_order.reshape(1, docs))


def solution(mesh):
    return jax.shard_map(
        local,
        mesh=mesh,
        in_specs=(
            P("ctx", "mp"),
            P("ctx", "mp"),
            P("mp", None),
            P("mp", None),
            P("mp", None),
            P(),
            P(),
        ),
        out_specs=P("ctx", "mp"),
        check_vma=False,
    )
```

time: 330 us -> 50.4 us (0.15)
  waiting for transfers between devices: 214 us -> 0 us
  matrix products: 42.6 us -> 0 us
  Pallas kernels: 0 us -> 41.7 us
  other arithmetic: 27.6 us -> 0 us
  local copies, waits for them, and re-layouts: 27.7 us -> 8.34 us
  between operations: 13.4 us -> 0.07 us
    psum x1 -> x0, waiting for transfers between devices: 153 us -> none  [local(): summed = lax.psum(stacked.astype(jnp.bfloat16), 'mp')]
    reduce_scatter x1 -> x0, waiting for transfers between devices: 61 us -> none  [local(): lax.psum_scatter(ordered.astype(jnp.bfloat16), 'ctx', scatter_dimension=0...]
    dot_general x8 -> x0, matrix products: 42.6 us -> none  [the longest x4 35.6 us: step(): lax.dot_general(weighted, right, (((0,), (0,)), ((), ())), preferred_elem...]
    pallas_call x0 -> x1, Pallas kernels: none -> 41.7 us  [local(): pl.pallas_call(kernel, out_shape=jax.ShapeDtypeStruct((own, nq), F32), in...]
    mul x4 -> x0, other arithmetic: 15.1 us -> none  [step(): member[:, :, None] * left[:, None, :]]
    unnamed x2 -> x11, local copies, waits for them, and re-layouts: 0.01 us -> 8.34 us
    reshape x1 -> x0, local copies, waits for them, and re-layouts: 7.89 us -> none  [doc_sums(): return total.reshape(doc_count, low_rank * low_rank)]
    gather x1 -> x0, local copies, waits for them, and re-layouts: 7.04 us -> none  [local(): ordered = jnp.take(doc_grad, doc_order, axis=0)]
  transfers between devices with their start and end apart: 2 -> 0, of which waited for: 2 -> 0; matrix products, arithmetic and copies ran while one was open for 1% -> 0% of each run, Pallas kernels for 0% -> 0%
where the time goes in v1:
time: 50.4 us; the launch traced here: 50.1 us
  Pallas kernels  41.7 us (83%)
  local copies, waits for them, and re-layouts  8.34 us (17%)
    pallas_call x1, Pallas kernels, local(): pl.pallas_call(kernel, out_shape=jax.ShapeDtypeStruct((own, nq), F32), in...  41.7 us
    unnamed x11, local copies, waits for them, and re-layouts  8.34 us

profile of v1, /device:TPU:1, one launch (start us, length us, event | category | flops | bytes accessed | tf_op | source)
XLA Modules:
  0.0 50.1 jit_solution(1468693265769192339)
XLA Ops:
  0.0 0.9 %copy.11.pout = bf16[160,64]{1,0:T(8,128)(2,1)S(1)} copy(bf16[160,64]{0,1:T(8,128)(2,1)} %param.10) | data formatting | bytes 40960 | tf_op args[3]
  0.9 1.1 %copy.10.pin = bf16[800,64]{1,0:T(8,128)(2,1)S(1)} copy(bf16[800,64]{0,1:T(8,128)(2,1)} %param.9) | data formatting | bytes 204800 | tf_op args[2]
  1.9 1.2 %copy.9.grad = bf16[1024,160]{1,0:T(8,128)(2,1)S(1)} copy(bf16[1024,160]{0,1:T(8,128)(2,1)} %param.8) | data formatting | bytes 655360 | tf_op args[1]
  3.1 0.0 copy-start.1
  3.1 0.0 copy-start.2
  3.2 3.0 %copy.8.hid = bf16[1024,800]{1,0:T(8,128)(2,1)S(1)} copy(bf16[1024,800]{0,1:T(8,128)(2,1)} %param.7) | data formatting | bytes 3276800 | tf_op args[0]
  6.2 0.0 copy-done.1
  6.2 0.0 copy-done.2
  6.2 0.0 copy-start
  6.2 1.6 %copy-done = bf16[256,4096]{1,0:T(8,128)(2,1)S(1)} copy-done((bf16[256,4096]{1,0:T(8,128)(2,1)S(1)}, bf16[256,4096]{1,0:T(8,128)(2,1)}, u32[]{:S(2)}) %copy-start) | copy-done | bytes 2097176
  7.8 41.7 %shard_map.73 = f32[16,256]{1,0:T(8,128)S(1)} custom-call(bf16[1024,800]{1,0:T(8,128)(2,1)S(1)} %copy.8.hid, bf16[1024,160]{1,0:T(8,128)(2,1)S(1)} %copy.9.grad, bf16[800,64]{1,0:T(8,128)(2,1)S(1)} %copy.10.pin, bf16[160,64]{1,0:T(8,128)(2,1)S(1)} %copy.11.pout, bf16[256,4096]{1,0:T(8,128)(2,1)S(1)} %copy-done, s32[1,256]{1,0:T(1,128)S(1)} %bitcast.2, ...), custom_call_target="tpu_custom_call" | custom-call | tf_op jit(solution)/shard_map/pallas_call | solution.py:239
  49.5 0.6 %copy.13 = f32[16,256]{1,0:T(8,128)} copy(f32[16,256]{1,0:T(8,128)S(1)} %shard_map.73) | data formatting | bytes 32768
Async XLA Ops:
  3.1 3.1 %copy-start.1 = (s32[256]{0:T(256)S(1)}, s32[256]{0:T(256)}, u32[]{:S(2)}) copy-start(s32[256]{0:T(256)} %param.12) | copy-start | bytes 3076
  3.1 3.1 %copy-start.2 = (s32[256]{0:T(256)S(1)}, s32[256]{0:T(256)}, u32[]{:S(2)}) copy-start(s32[256]{0:T(256)} %param.13) | copy-start | bytes 3076
  6.2 1.6 %copy-start = (bf16[256,4096]{1,0:T(8,128)(2,1)S(1)}, bf16[256,4096]{1,0:T(8,128)(2,1)}, u32[]{:S(2)}) copy-start(bf16[256,4096]{1,0:T(8,128)(2,1)} %qry.1) | copy-start | bytes 6291460

commit v2 on v1

--- a/solution.py
+++ b/solution.py
@@ -32,14 +32,14 @@
 
 def kernel(
     hid, grad, pin, pout, qry, lens, order, out,
-    vhid, vgrad, vpin, vpout, vq, qp, member, scale,
+    vhid, vgrad, vpin, vpout, vlens, vorder, vq, qp, member, scale,
     lsend, lrecv, l2send, l2recv, rsend, rrecv, r2send, r2recv, gsend, grecv, fsend, frecv,
     load_sem, send_sem, recv_sem,
 ):
     mp, ctx = lax.axis_index("mp"), lax.axis_index("ctx")
     z, x = mp // NX, lax.rem(mp, NX)
     y, core = ctx // 2, lax.rem(ctx, 2)
-    tok = vhid.shape[0]
+    tok = vhid.shape[1]
     half = tok // 2
     quarter = tok // 4
     docs = member.shape[0]
@@ -60,22 +60,26 @@
                 yield lax.rem(y + s, NY) * 2 + (core if c == 0 else 1 - core)
         yield y * 2 + 1 - core
 
+    barrier = pltpu.get_barrier_semaphore()
+    for s in Z_OFF:
+        pl.semaphore_signal(barrier, inc=1, device_id=z_peer(s), device_id_type=MESH)
+    for peer in ctx_peers():
+        pl.semaphore_signal(barrier, inc=1, device_id=(mp, peer), device_id_type=MESH)
+    for s in X_OFF:
+        pl.semaphore_signal(barrier, inc=1, device_id=x_peer(s), device_id_type=MESH)
+
     loads = [
         pltpu.make_async_copy(grad, vgrad, load_sem.at[0]),
         pltpu.make_async_copy(pout, vpout, load_sem.at[1]),
         pltpu.make_async_copy(pin, vpin, load_sem.at[2]),
-        pltpu.make_async_copy(hid.at[pl.ds(0, half)], vhid.at[pl.ds(0, half)], load_sem.at[3]),
-        pltpu.make_async_copy(hid.at[pl.ds(half, half)], vhid.at[pl.ds(half, half)], load_sem.at[4]),
-        pltpu.make_async_copy(qry, vq, load_sem.at[5]),
+        pltpu.make_async_copy(hid.at[:, pl.ds(0, half)], vhid.at[:, pl.ds(0, half)], load_sem.at[3]),
+        pltpu.make_async_copy(hid.at[:, pl.ds(half, half)], vhid.at[:, pl.ds(half, half)], load_sem.at[4]),
+        pltpu.make_async_copy(lens, vlens, load_sem.at[5]),
+        pltpu.make_async_copy(order, vorder, load_sem.at[6]),
+        pltpu.make_async_copy(qry, vq, load_sem.at[7]),
     ]
     for load in loads:
         load.start()
-
-    barrier = pltpu.get_barrier_semaphore()
-    for dz, dx in MP_OFF:
-        pl.semaphore_signal(barrier, inc=1, device_id=mp_peer(dz, dx), device_id_type=MESH)
-    for peer in ctx_peers():
-        pl.semaphore_signal(barrier, inc=1, device_id=(mp, peer), device_id_type=MESH)
 
     started = []
 
@@ -92,24 +96,21 @@
 
     loads[0].wait()
     loads[1].wait()
-    right = lax.dot_general(vpout[...], vgrad[...], (((0,), (1,)), ((), ())), preferred_element_type=F32)
+    right = jnp.dot(vpout[...], vgrad[...], preferred_element_type=F32)
     right = right.astype(BF16)
     for p in range(NX):
         rsend[p] = right[p * XR:(p + 1) * XR]
-    pl.semaphore_wait(barrier, NMP - 1 + NCTX - 1)
-    for s in X_OFF:
-        send(rsend.at[lax.rem(x + s, NX)], rrecv.at[x], 0, x_peer(s))
-
     loads[2].wait()
     for b in range(2):
         loads[3 + b].wait()
-        left = lax.dot_general(
-            vpin[...], vhid[pl.ds(b * half, half), :], (((0,), (1,)), ((), ())), preferred_element_type=F32
-        )
+        left = jnp.dot(vpin[...], vhid[:, pl.ds(b * half, half)], preferred_element_type=F32)
         for p in range(NZ):
             rows = left[p * ZL:(p + 1) * ZL]
             slot = jnp.concatenate([rows[:, :quarter], rows[:, quarter:]], axis=0)
             lsend[p, :, b * quarter:(b + 1) * quarter] = slot.astype(BF16)
+    pl.semaphore_wait(barrier, NZ - 1 + NX - 1 + NCTX - 1)
+    for s in X_OFF:
+        send(rsend.at[lax.rem(x + s, NX)], rrecv.at[x], 0, x_peer(s))
     for s in Z_OFF:
         send(lsend.at[lax.rem(z + s, NZ)], lrecv.at[z], 1, z_peer(s))
     rrecv[x] = rsend[x]
@@ -117,8 +118,10 @@
 
     lane = lax.broadcasted_iota(jnp.int32, (docs, docs), 1)
     row = lax.broadcasted_iota(jnp.int32, (docs, docs), 0)
-    length = lens[...].astype(F32)
-    index = order[...].astype(F32)
+    loads[5].wait()
+    loads[6].wait()
+    length = vlens[...].astype(F32).reshape(1, docs)
+    index = vorder[...].astype(F32).reshape(1, docs)
     doc = jnp.sum(jnp.where(lane == row, index, 0.0), axis=1, keepdims=True)
     lane_f = lane.astype(F32)
     first = jnp.sum(jnp.where(lane_f < doc, length, 0.0), axis=1, keepdims=True)
@@ -145,16 +148,18 @@
         send(l2send, l2recv.at[x], 3, x_peer(s))
     l2recv[x] = l2send[...]
 
-    loads[5].wait()
+    loads[7].wait()
     wide = ZL * RANK
     cut = ZL * XR
-    to = lax.broadcasted_iota(jnp.int32, (wide, wide), 1)
-    at = lax.broadcasted_iota(jnp.int32, (wide, wide), 0)
+    to = lax.broadcasted_iota(jnp.int32, (wide, wide), 0)
+    at = lax.broadcasted_iota(jnp.int32, (wide, wide), 1)
     source = (to % cut) // XR * RANK + to // cut * XR + to % XR
     moved = jnp.where(at == source, 1.0, 0.0).astype(BF16)
     for p in range(NZ):
-        piece = jnp.dot(vq[:, p * wide:(p + 1) * wide], moved, preferred_element_type=F32)
-        qp[:, p * wide:(p + 1) * wide] = piece.astype(BF16)
+        piece = lax.dot_general(
+            moved, vq[:, p * wide:(p + 1) * wide], (((1,), (1,)), ((), ())), preferred_element_type=F32
+        )
+        qp[p * wide:(p + 1) * wide] = piece.astype(BF16)
 
     arrived(l2recv, NX - 1, 3)
     total = l2recv[0].astype(F32)
@@ -196,7 +201,7 @@
     arrived(frecv, NMP - 1, 5)
 
     grads = jnp.concatenate([frecv[p] for p in range(NMP)], axis=1)
-    out[...] = lax.dot_general(grads, qp[...], (((1,), (1,)), ((), ())), preferred_element_type=F32)
+    out[...] = jnp.dot(grads, qp[...], preferred_element_type=F32)
 
     for part, phase in started:
         pltpu.make_async_copy(part, part, send_sem.at[phase]).wait()
@@ -209,15 +214,17 @@
     docs = lengths.shape[0]
     own = docs // NCTX
     cut = ZL * XR
-    anywhere = pl.BlockSpec(memory_space=pl.ANY)
+    hbm = pl.BlockSpec(memory_space=pltpu.HBM)
     vmem = pl.BlockSpec(memory_space=pltpu.VMEM)
     scratch = [
-        pltpu.VMEM((tok, hid), BF16),
-        pltpu.VMEM((tok, feat), BF16),
-        pltpu.VMEM((hid, RANK), BF16),
-        pltpu.VMEM((feat, RANK), BF16),
+        pltpu.VMEM((hid, tok), BF16),
+        pltpu.VMEM((feat, tok), BF16),
+        pltpu.VMEM((RANK, hid), BF16),
+        pltpu.VMEM((RANK, feat), BF16),
+        pltpu.VMEM((docs,), jnp.int32),
+        pltpu.VMEM((docs,), jnp.int32),
         pltpu.VMEM((nq, wide), BF16),
-        pltpu.VMEM((nq, wide), BF16),
+        pltpu.VMEM((wide, nq), BF16),
         pltpu.VMEM((docs, tok), BF16),
         pltpu.VMEM((docs, cut), F32),
         pltpu.VMEM((NZ, 2 * ZL, tok // 2), BF16),
@@ -232,20 +239,20 @@
         pltpu.VMEM((NCTX, own, cut), BF16),
         pltpu.VMEM((own, cut), BF16),
         pltpu.VMEM((NMP, own, cut), BF16),
-        pltpu.SemaphoreType.DMA((6,)),
+        pltpu.SemaphoreType.DMA((8,)),
         pltpu.SemaphoreType.DMA((6,)),
         pltpu.SemaphoreType.DMA((6,)),
     ]
     return pl.pallas_call(
         kernel,
         out_shape=jax.ShapeDtypeStruct((own, nq), F32),
-        in_specs=[anywhere] * 5 + [vmem] * 2,
+        in_specs=[hbm] * 7,
         out_specs=vmem,
         scratch_shapes=scratch,
         compiler_params=pltpu.CompilerParams(
-            collective_id=0, has_side_effects=True, vmem_limit_bytes=40 * 1024 * 1024
+            collective_id=0, has_side_effects=True, vmem_limit_bytes=60 * 1024 * 1024
         ),
-    )(hidden_act, out_grad, proj_in, proj_out, queries, lengths.reshape(1, docs), doc_order.reshape(1, docs))
+    )(hidden_act.T, out_grad.T, proj_in.T, proj_out.T, queries, lengths, doc_order)
 
 
 def solution(mesh):

time: 50.4 us -> 40.3 us (0.80)
  local copies, waits for them, and re-layouts: 8.34 us -> 1.32 us
  Pallas kernels: 41.7 us -> 38.8 us
    unnamed x11 -> x1, local copies, waits for them, and re-layouts: 8.34 us -> 1.32 us
    pallas_call x1, Pallas kernels: 41.7 us -> 38.8 us  [local(): pl.pallas_call(kernel, out_shape=jax.ShapeDtypeStruct((own, nq), F32), in...]
where the time goes in v2:
time: 40.3 us; the launch traced here: 40.1 us
  Pallas kernels  38.8 us (96%)
  local copies, waits for them, and re-layouts  1.32 us (3%)
    pallas_call x1, Pallas kernels, local(): pl.pallas_call(kernel, out_shape=jax.ShapeDtypeStruct((own, nq), F32), in...  38.8 us
    unnamed x1, local copies, waits for them, and re-layouts  1.32 us

profile of v2, /device:TPU:1, one launch (start us, length us, event | category | flops | bytes accessed | tf_op | source)
XLA Modules:
  0.0 40.1 jit_solution(5935079602270350245)
XLA Ops:
  0.0 38.8 %shard_map.73 = f32[16,256]{1,0:T(8,128)} custom-call(bf16[800,1024]{1,0:T(8,128)(2,1)} %bitcast.4, bf16[160,1024]{1,0:T(8,128)(2,1)} %bitcast.5, bf16[64,800]{1,0:T(8,128)(2,1)} %bitcast.6, bf16[64,160]{1,0:T(8,128)(2,1)} %bitcast.7, bf16[256,4096]{1,0:T(8,128)(2,1)} %qry.1, s32[256]{0:T(256)} %lens.1, s32[256]{0:T(256)} %order.1), custom_call_target="tpu_custom_call" | custom-call | tf_op jit(solution)/shard_map/pallas_call | solution.py:246
  38.8 1.3 %copy.9 = f32[16,256]{1,0:T(8,128)} copy(f32[16,256]{1,0:T(8,128)} %shard_map.73) | data formatting | bytes 32768

commit v3 on v2

--- a/solution.py
+++ b/solution.py
@@ -39,6 +39,8 @@
     mp, ctx = lax.axis_index("mp"), lax.axis_index("ctx")
     z, x = mp // NX, lax.rem(mp, NX)
     y, core = ctx // 2, lax.rem(ctx, 2)
+    odd = lax.rem(z, 2)
+    twin = z + 1 - 2 * odd
     tok = vhid.shape[1]
     half = tok // 2
     quarter = tok // 4
@@ -51,6 +53,9 @@
     def x_peer(s):
         return (z * NX + lax.rem(x + s, NX), ctx)
 
+    def pair_peer(s):
+        return (twin * NX + lax.rem(x + s, NX), ctx)
+
     def mp_peer(dz, dx):
         return (lax.rem(z + dz, NZ) * NX + lax.rem(x + dx, NX), ctx)
 
@@ -61,25 +66,36 @@
         yield y * 2 + 1 - core
 
     barrier = pltpu.get_barrier_semaphore()
+    far, near = [], []
     for s in Z_OFF:
-        pl.semaphore_signal(barrier, inc=1, device_id=z_peer(s), device_id_type=MESH)
-    for peer in ctx_peers():
-        pl.semaphore_signal(barrier, inc=1, device_id=(mp, peer), device_id_type=MESH)
+        (far if hops(s, NZ) > 2 else near).append((hops(s, NZ), z_peer(s)))
+    for s in Y_OFF:
+        for peer in (core, 1 - core):
+            device = (mp, lax.rem(y + s, NY) * 2 + peer)
+            (far if hops(s, NY) > 2 else near).append((hops(s, NY), device))
     for s in X_OFF:
-        pl.semaphore_signal(barrier, inc=1, device_id=x_peer(s), device_id_type=MESH)
+        near.append((hops(s, NX), x_peer(s)))
+        near.append((hops(s, NX) + 1, pair_peer(s)))
+    near.append((0, (mp, y * 2 + 1 - core)))
+
+    def greet(devices):
+        for _, device in sorted(devices, key=lambda d: -d[0]):
+            pl.semaphore_signal(barrier, inc=1, device_id=device, device_id_type=MESH)
 
     loads = [
         pltpu.make_async_copy(grad, vgrad, load_sem.at[0]),
         pltpu.make_async_copy(pout, vpout, load_sem.at[1]),
+        pltpu.make_async_copy(hid.at[:, pl.ds(0, half)], vhid.at[:, pl.ds(0, half)], load_sem.at[3]),
         pltpu.make_async_copy(pin, vpin, load_sem.at[2]),
-        pltpu.make_async_copy(hid.at[:, pl.ds(0, half)], vhid.at[:, pl.ds(0, half)], load_sem.at[3]),
         pltpu.make_async_copy(hid.at[:, pl.ds(half, half)], vhid.at[:, pl.ds(half, half)], load_sem.at[4]),
         pltpu.make_async_copy(lens, vlens, load_sem.at[5]),
         pltpu.make_async_copy(order, vorder, load_sem.at[6]),
         pltpu.make_async_copy(qry, vq, load_sem.at[7]),
     ]
-    for load in loads:
+    greet(far)
+    for load in loads[:5]:
         load.start()
+    greet(near)
 
     started = []
 
@@ -96,24 +112,30 @@
 
     loads[0].wait()
     loads[1].wait()
-    right = jnp.dot(vpout[...], vgrad[...], preferred_element_type=F32)
-    right = right.astype(BF16)
+    right = jnp.dot(vpout[...], vgrad[...], preferred_element_type=F32).astype(BF16)
     for p in range(NX):
-        rsend[p] = right[p * XR:(p + 1) * XR]
-    loads[2].wait()
+        for h in range(2):
+            rsend[2 * p + h] = right[p * XR:(p + 1) * XR, h * half:(h + 1) * half]
+
+    loads[3].wait()
     for b in range(2):
-        loads[3 + b].wait()
+        loads[2 + 2 * b].wait()
         left = jnp.dot(vpin[...], vhid[:, pl.ds(b * half, half)], preferred_element_type=F32)
         for p in range(NZ):
             rows = left[p * ZL:(p + 1) * ZL]
             slot = jnp.concatenate([rows[:, :quarter], rows[:, quarter:]], axis=0)
             lsend[p, :, b * quarter:(b + 1) * quarter] = slot.astype(BF16)
-    pl.semaphore_wait(barrier, NZ - 1 + NX - 1 + NCTX - 1)
+    pl.semaphore_wait(barrier, NZ - 1 + 2 * (NX - 1) + NCTX - 1)
     for s in X_OFF:
-        send(rsend.at[lax.rem(x + s, NX)], rrecv.at[x], 0, x_peer(s))
+        to = 2 * lax.rem(x + s, NX)
+        send(rsend.at[to + 1 - odd], rrecv.at[2 * x + odd], 0, pair_peer(s))
+        send(rsend.at[to + odd], rrecv.at[2 * x + odd], 0, x_peer(s))
+    send(rsend.at[2 * x + 1 - odd], rrecv.at[2 * x + odd], 0, (twin * NX + x, ctx))
     for s in Z_OFF:
         send(lsend.at[lax.rem(z + s, NZ)], lrecv.at[z], 1, z_peer(s))
-    rrecv[x] = rsend[x]
+    for load in loads[5:]:
+        load.start()
+    rrecv[2 * x + odd] = rsend[2 * x + odd]
     lrecv[z] = lsend[z]
 
     lane = lax.broadcasted_iota(jnp.int32, (docs, docs), 1)
@@ -130,9 +152,9 @@
     place = (lax.broadcasted_iota(jnp.int32, (docs, tok), 1) + ctx * tok).astype(F32)
     member[...] = jnp.where((place >= first) & (place < first + size), 1.0, 0.0).astype(BF16)
 
-    arrived(rrecv, NX - 1, 0)
+    arrived(rrecv, 2 * NX - 1, 0)
     total = rrecv[0].astype(F32)
-    for p in range(1, NX):
+    for p in range(1, 2 * NX):
         total += rrecv[p].astype(F32)
     r2send[...] = total.astype(BF16)
     for s in Z_OFF:
@@ -167,15 +189,17 @@
         total += l2recv[p].astype(F32)
     left = total.astype(BF16).astype(F32)
     arrived(r2recv, NZ - 1, 2)
-    total = r2recv[0].astype(F32)
-    for p in range(1, NZ):
-        total += r2recv[p].astype(F32)
-    right = total.astype(BF16).astype(F32)
+    right = []
+    for h in range(2):
+        total = r2recv[h].astype(F32)
+        for p in range(h + 2, NZ, 2):
+            total += r2recv[p].astype(F32)
+        right.append(total.astype(BF16).astype(F32))
     sums = jnp.zeros((docs, cut), F32)
     for b in range(2):
         for h in range(2):
             start = b * half + h * quarter
-            piece = right[:, start:start + quarter]
+            piece = right[b][:, h * quarter:(h + 1) * quarter]
             outer = jnp.concatenate(
                 [left[h * ZL + i:h * ZL + i + 1, b * quarter:(b + 1) * quarter] * piece for i in range(ZL)], axis=0
             )
@@ -231,10 +255,10 @@
         pltpu.VMEM((NZ, 2 * ZL, tok // 2), BF16),
         pltpu.VMEM((2 * ZL, tok // 2), BF16),
         pltpu.VMEM((NX, 2 * ZL, tok // 2), BF16),
-        pltpu.VMEM((NX, XR, tok), BF16),
-        pltpu.VMEM((NX, XR, tok), BF16),
-        pltpu.VMEM((XR, tok), BF16),
-        pltpu.VMEM((NZ, XR, tok), BF16),
+        pltpu.VMEM((2 * NX, XR, tok // 2), BF16),
+        pltpu.VMEM((2 * NX, XR, tok // 2), BF16),
+        pltpu.VMEM((XR, tok // 2), BF16),
+        pltpu.VMEM((NZ, XR, tok // 2), BF16),
         pltpu.VMEM((NCTX, own, cut), BF16),
         pltpu.VMEM((NCTX, own, cut), BF16),
         pltpu.VMEM((own, cut), BF16),
@@ -245,14 +269,17 @@
     ]
     return pl.pallas_call(
         kernel,
-        out_shape=jax.ShapeDtypeStruct((own, nq), F32),
+        out_shape=pltpu.VMEM((own, nq), F32),
         in_specs=[hbm] * 7,
         out_specs=vmem,
         scratch_shapes=scratch,
         compiler_params=pltpu.CompilerParams(
-            collective_id=0, has_side_effects=True, vmem_limit_bytes=60 * 1024 * 1024
+            collective_id=0, has_side_effects=True, vmem_limit_bytes=40 * 1024 * 1024
         ),
-    )(hidden_act.T, out_grad.T, proj_in.T, proj_out.T, queries, lengths, doc_order)
+    )(*[
+        pltpu.with_memory_space_constraint(a, pltpu.HBM)
+        for a in (hidden_act.T, out_grad.T, proj_in.T, proj_out.T, queries, lengths, doc_order)
+    ])
 
 
 def solution(mesh):

time: 40.3 us -> 39.4 us (0.978)
  local copies, waits for them, and re-layouts: 1.32 us -> 0.61 us
    unnamed x1, local copies, waits for them, and re-layouts: 1.32 us -> 0.61 us
where the time goes in v3:
time: 39.4 us; the launch traced here: 39.3 us
  Pallas kernels  38.7 us (98%)
  local copies, waits for them, and re-layouts  0.61 us (2%)
    pallas_call x1, Pallas kernels, local(): pl.pallas_call(kernel, out_shape=pltpu.VMEM((own, nq), F32), in_specs=[hb...  38.7 us

profile of v3, /device:TPU:1, one launch (start us, length us, event | category | flops | bytes accessed | tf_op | source)
XLA Modules:
  0.0 39.3 jit_solution(1583631445449724716)
XLA Ops:
  0.0 38.7 %shard_map.73 = f32[16,256]{1,0:T(8,128)S(1)} custom-call(bf16[800,1024]{1,0:T(8,128)(2,1)} %bitcast.4, bf16[160,1024]{1,0:T(8,128)(2,1)} %bitcast.5, bf16[64,800]{1,0:T(8,128)(2,1)} %bitcast.6, bf16[64,160]{1,0:T(8,128)(2,1)} %bitcast.7, bf16[256,4096]{1,0:T(8,128)(2,1)} %qry.1, s32[256]{0:T(256)} %lens.1, s32[256]{0:T(256)} %order.1), custom_call_target="tpu_custom_call" | custom-call | tf_op jit(solution)/shard_map/pallas_call | solution.py:270
  38.7 0.6 %copy.9 = f32[16,256]{1,0:T(8,128)} copy(f32[16,256]{1,0:T(8,128)S(1)} %shard_map.73) | data formatting | bytes 32768

commit v4 on v3

--- a/solution.py
+++ b/solution.py
@@ -39,8 +39,9 @@
     mp, ctx = lax.axis_index("mp"), lax.axis_index("ctx")
     z, x = mp // NX, lax.rem(mp, NX)
     y, core = ctx // 2, lax.rem(ctx, 2)
-    odd = lax.rem(z, 2)
-    twin = z + 1 - 2 * odd
+    odd = lax.rem(z + core, 2)
+    twin = lax.rem(z + NZ + 1 - 2 * odd, NZ)
+    place_z = lax.rem(z + core, NZ)
     tok = vhid.shape[1]
     half = tok // 2
     quarter = tok // 4
@@ -158,8 +159,8 @@
         total += rrecv[p].astype(F32)
     r2send[...] = total.astype(BF16)
     for s in Z_OFF:
-        send(r2send, r2recv.at[z], 2, z_peer(s))
-    r2recv[z] = r2send[...]
+        send(r2send, r2recv.at[place_z], 2, z_peer(s))
+    r2recv[place_z] = r2send[...]
 
     arrived(lrecv, NZ - 1, 1)
     total = lrecv[0].astype(F32)

time: 39.4 us -> 37.8 us (0.959)
  Pallas kernels: 38.7 us -> 37 us
    pallas_call x1, Pallas kernels: 38.7 us -> 37 us  [local(): pl.pallas_call(kernel, out_shape=pltpu.VMEM((own, nq), F32), in_specs=[hb...]
where the time goes in v4:
time: 37.8 us; the launch traced here: 37.6 us
  Pallas kernels  37 us (98%)
  local copies, waits for them, and re-layouts  0.61 us (2%)
    pallas_call x1, Pallas kernels, local(): pl.pallas_call(kernel, out_shape=pltpu.VMEM((own, nq), F32), in_specs=[hb...  37 us

profile of v4, /device:TPU:1, one launch (start us, length us, event | category | flops | bytes accessed | tf_op | source)
XLA Modules:
  0.0 37.6 jit_solution(8078769374464936924)
XLA Ops:
  0.0 37.0 %shard_map.73 = f32[16,256]{1,0:T(8,128)S(1)} custom-call(bf16[800,1024]{1,0:T(8,128)(2,1)} %bitcast.4, bf16[160,1024]{1,0:T(8,128)(2,1)} %bitcast.5, bf16[64,800]{1,0:T(8,128)(2,1)} %bitcast.6, bf16[64,160]{1,0:T(8,128)(2,1)} %bitcast.7, bf16[256,4096]{1,0:T(8,128)(2,1)} %qry.1, s32[256]{0:T(256)} %lens.1, s32[256]{0:T(256)} %order.1), custom_call_target="tpu_custom_call" | custom-call | tf_op jit(solution)/shard_map/pallas_call | solution.py:271
  37.0 0.6 %copy.9 = f32[16,256]{1,0:T(8,128)} copy(f32[16,256]{1,0:T(8,128)S(1)} %shard_map.73) | data formatting | bytes 32768

commit v5 on v4

--- a/solution.py
+++ b/solution.py
@@ -29,10 +29,12 @@
     key=lambda o: (-hops(o[0], NZ) - hops(o[1], NX), o),
 )
 
+FAR = sum(hops(dz, NZ) + hops(dx, NX) > 3 for dz, dx in MP_OFF)
+
 
 def kernel(
     hid, grad, pin, pout, qry, lens, order, out,
-    vhid, vgrad, vpin, vpout, vlens, vorder, vq, qp, member, scale,
+    vhid, vgrad, vpin, vpout, vlens, vorder, vq, qp, qs, member, scale,
     lsend, lrecv, l2send, l2recv, rsend, rrecv, r2send, r2recv, gsend, grecv, fsend, frecv,
     load_sem, send_sem, recv_sem,
 ):
@@ -67,6 +69,10 @@
         yield y * 2 + 1 - core
 
     barrier = pltpu.get_barrier_semaphore()
+    mp_peers = [mp_peer(dz, dx) for dz, dx in MP_OFF]
+    sources = [lax.rem(z + NZ - dz, NZ) * NX + lax.rem(x + NX - dx, NX) for dz, dx in MP_OFF] + [mp]
+    ctx_all = list(ctx_peers())
+    z_peers, x_peers, pair_peers = [z_peer(s) for s in Z_OFF], [x_peer(s) for s in X_OFF], [pair_peer(s) for s in X_OFF]
     far, near = [], []
     for s in Z_OFF:
         (far if hops(s, NZ) > 2 else near).append((hops(s, NZ), z_peer(s)))
@@ -132,8 +138,8 @@
         send(rsend.at[to + 1 - odd], rrecv.at[2 * x + odd], 0, pair_peer(s))
         send(rsend.at[to + odd], rrecv.at[2 * x + odd], 0, x_peer(s))
     send(rsend.at[2 * x + 1 - odd], rrecv.at[2 * x + odd], 0, (twin * NX + x, ctx))
-    for s in Z_OFF:
-        send(lsend.at[lax.rem(z + s, NZ)], lrecv.at[z], 1, z_peer(s))
+    for s, peer in zip(Z_OFF, z_peers):
+        send(lsend.at[lax.rem(z + s, NZ)], lrecv.at[z], 1, peer)
     for load in loads[5:]:
         load.start()
     rrecv[2 * x + odd] = rsend[2 * x + odd]
@@ -158,8 +164,8 @@
     for p in range(1, 2 * NX):
         total += rrecv[p].astype(F32)
     r2send[...] = total.astype(BF16)
-    for s in Z_OFF:
-        send(r2send, r2recv.at[place_z], 2, z_peer(s))
+    for peer in z_peers:
+        send(r2send, r2recv.at[place_z], 2, peer)
     r2recv[place_z] = r2send[...]
 
     arrived(lrecv, NZ - 1, 1)
@@ -167,23 +173,11 @@
     for p in range(1, NZ):
         total += lrecv[p].astype(F32)
     l2send[...] = total.astype(BF16)
-    for s in X_OFF:
-        send(l2send, l2recv.at[x], 3, x_peer(s))
+    for peer in x_peers:
+        send(l2send, l2recv.at[x], 3, peer)
     l2recv[x] = l2send[...]
 
-    loads[7].wait()
-    wide = ZL * RANK
     cut = ZL * XR
-    to = lax.broadcasted_iota(jnp.int32, (wide, wide), 0)
-    at = lax.broadcasted_iota(jnp.int32, (wide, wide), 1)
-    source = (to % cut) // XR * RANK + to // cut * XR + to % XR
-    moved = jnp.where(at == source, 1.0, 0.0).astype(BF16)
-    for p in range(NZ):
-        piece = lax.dot_general(
-            moved, vq[:, p * wide:(p + 1) * wide], (((1,), (1,)), ((), ())), preferred_element_type=F32
-        )
-        qp[p * wide:(p + 1) * wide] = piece.astype(BF16)
-
     arrived(l2recv, NX - 1, 3)
     total = l2recv[0].astype(F32)
     for p in range(1, NX):
@@ -211,7 +205,7 @@
     sums = sums.astype(BF16)
     for p in range(NCTX):
         gsend[p] = sums[p * own:(p + 1) * own]
-    for peer in ctx_peers():
+    for peer in ctx_all:
         send(gsend.at[peer], grecv.at[ctx], 4, (mp, peer))
     grecv[ctx] = gsend[ctx]
 
@@ -220,13 +214,31 @@
     for p in range(1, NCTX):
         total += grecv[p].astype(F32)
     fsend[...] = (total * scale[pl.ds(ctx * own, own), :]).astype(BF16)
-    for dz, dx in MP_OFF:
-        send(fsend, frecv.at[mp], 5, mp_peer(dz, dx))
-    frecv[mp] = fsend[...]
-    arrived(frecv, NMP - 1, 5)
-
-    grads = jnp.concatenate([frecv[p] for p in range(NMP)], axis=1)
-    out[...] = jnp.dot(grads, qp[...], preferred_element_type=F32)
+    for slot, peer in enumerate(mp_peers):
+        send(fsend, frecv.at[slot], 5 if slot < FAR else 6, peer)
+    frecv[NMP - 1] = fsend[...]
+
+    loads[7].wait()
+    wide = ZL * RANK
+    to = lax.broadcasted_iota(jnp.int32, (wide, wide), 0)
+    at = lax.broadcasted_iota(jnp.int32, (wide, wide), 1)
+    source = (to % cut) // XR * RANK + to // cut * XR + to % XR
+    moved = jnp.where(at == source, 1.0, 0.0).astype(BF16)
+    for p in range(NZ):
+        piece = lax.dot_general(
+            moved, vq[:, p * wide:(p + 1) * wide], (((1,), (1,)), ((), ())), preferred_element_type=F32
+        )
+        qp[p * wide:(p + 1) * wide] = piece.astype(BF16)
+
+    for slot, source in enumerate(sources):
+        qs[slot * cut:(slot + 1) * cut] = qp[pl.ds(pl.multiple_of(source * cut, cut), cut), :]
+
+    arrived(frecv.at[pl.ds(FAR, NMP - 1 - FAR)], NMP - 1 - FAR, 6)
+    grads = jnp.concatenate([frecv[p] for p in range(FAR, NMP)], axis=1)
+    part_near = jnp.dot(grads, qs[FAR * cut:], preferred_element_type=F32)
+    arrived(frecv, FAR, 5)
+    grads = jnp.concatenate([frecv[p] for p in range(FAR)], axis=1)
+    out[...] = part_near + jnp.dot(grads, qs[:FAR * cut], preferred_element_type=F32)
 
     for part, phase in started:
         pltpu.make_async_copy(part, part, send_sem.at[phase]).wait()
@@ -250,6 +262,7 @@
         pltpu.VMEM((docs,), jnp.int32),
         pltpu.VMEM((nq, wide), BF16),
         pltpu.VMEM((wide, nq), BF16),
+        pltpu.VMEM((wide, nq), BF16),
         pltpu.VMEM((docs, tok), BF16),
         pltpu.VMEM((docs, cut), F32),
         pltpu.VMEM((NZ, 2 * ZL, tok // 2), BF16),
@@ -265,8 +278,8 @@
         pltpu.VMEM((own, cut), BF16),
         pltpu.VMEM((NMP, own, cut), BF16),
         pltpu.SemaphoreType.DMA((8,)),
-        pltpu.SemaphoreType.DMA((6,)),
-        pltpu.SemaphoreType.DMA((6,)),
+        pltpu.SemaphoreType.DMA((7,)),
+        pltpu.SemaphoreType.DMA((7,)),
     ]
     return pl.pallas_call(
         kernel,

time: 37.8 us -> 37.8 us (level)
  no operation moved by 1% of the time
where the time goes in v5:
time: 37.8 us; the launch traced here: 37.6 us
  Pallas kernels  37 us (98%)
  local copies, waits for them, and re-layouts  0.61 us (2%)
    pallas_call x1, Pallas kernels, local(): pl.pallas_call(kernel, out_shape=pltpu.VMEM((own, nq), F32), in_specs=[hb...  37 us

profile of v5, /device:TPU:1, one launch (start us, length us, event | category | flops | bytes accessed | tf_op | source)
XLA Modules:
  0.0 37.6 jit_solution(17379549337486900867)
XLA Ops:
  0.0 37.0 %shard_map.73 = f32[16,256]{1,0:T(8,128)S(1)} custom-call(bf16[800,1024]{1,0:T(8,128)(2,1)} %bitcast.4, bf16[160,1024]{1,0:T(8,128)(2,1)} %bitcast.5, bf16[64,800]{1,0:T(8,128)(2,1)} %bitcast.6, bf16[64,160]{1,0:T(8,128)(2,1)} %bitcast.7, bf16[256,4096]{1,0:T(8,128)(2,1)} %qry.1, s32[256]{0:T(256)} %lens.1, s32[256]{0:T(256)} %order.1), custom_call_target="tpu_custom_call" | custom-call | tf_op jit(solution)/shard_map/pallas_call | solution.py:284
  37.0 0.6 %copy.9 = f32[16,256]{1,0:T(8,128)} copy(f32[16,256]{1,0:T(8,128)S(1)} %shard_map.73) | data formatting | bytes 32768

commit v6 on v4

--- a/solution.py
+++ b/solution.py
@@ -93,10 +93,10 @@
         pltpu.make_async_copy(order, vorder, load_sem.at[6]),
         pltpu.make_async_copy(qry, vq, load_sem.at[7]),
     ]
-    greet(far)
+    greet(far + [(9, d) for h, d in near if h == 3])
     for load in loads[:5]:
         load.start()
-    greet(near)
+    greet([n for n in near if n[0] != 3])
 
     started = []
 

time: 37.8 us -> 37.7 us (level)
  no operation moved by 1% of the time
where the time goes in v6:
time: 37.7 us; the launch traced here: 37.6 us
  Pallas kernels  36.9 us (98%)
  local copies, waits for them, and re-layouts  0.61 us (2%)
    pallas_call x1, Pallas kernels, local(): pl.pallas_call(kernel, out_shape=pltpu.VMEM((own, nq), F32), in_specs=[hb...  36.9 us

profile of v6, /device:TPU:1, one launch (start us, length us, event | category | flops | bytes accessed | tf_op | source)
XLA Modules:
  0.0 37.6 jit_solution(11305948915302067856)
XLA Ops:
  0.0 36.9 %shard_map.73 = f32[16,256]{1,0:T(8,128)S(1)} custom-call(bf16[800,1024]{1,0:T(8,128)(2,1)} %bitcast.4, bf16[160,1024]{1,0:T(8,128)(2,1)} %bitcast.5, bf16[64,800]{1,0:T(8,128)(2,1)} %bitcast.6, bf16[64,160]{1,0:T(8,128)(2,1)} %bitcast.7, bf16[256,4096]{1,0:T(8,128)(2,1)} %qry.1, s32[256]{0:T(256)} %lens.1, s32[256]{0:T(256)} %order.1), custom_call_target="tpu_custom_call" | custom-call | tf_op jit(solution)/shard_map/pallas_call | solution.py:271
  37.0 0.6 %copy.9 = f32[16,256]{1,0:T(8,128)} copy(f32[16,256]{1,0:T(8,128)S(1)} %shard_map.73) | data formatting | bytes 32768

commit v7 on v5

--- a/solution.py
+++ b/solution.py
@@ -29,7 +29,7 @@
     key=lambda o: (-hops(o[0], NZ) - hops(o[1], NX), o),
 )
 
-FAR = sum(hops(dz, NZ) + hops(dx, NX) > 3 for dz, dx in MP_OFF)
+FAR = sum(hops(dz, NZ) + hops(dx, NX) > 4 for dz, dx in MP_OFF)
 
 
 def kernel(
@@ -99,10 +99,10 @@
         pltpu.make_async_copy(order, vorder, load_sem.at[6]),
         pltpu.make_async_copy(qry, vq, load_sem.at[7]),
     ]
-    greet(far)
+    greet(far + [(9, d) for h, d in near if h == 3])
     for load in loads[:5]:
         load.start()
-    greet(near)
+    greet([n for n in near if n[0] != 3])
 
     started = []
 

time: 37.8 us -> 37.8 us (level)
  no operation moved by 1% of the time
where the time goes in v7:
time: 37.8 us; the launch traced here: 37.6 us
  Pallas kernels  37 us (98%)
  local copies, waits for them, and re-layouts  0.61 us (2%)
    pallas_call x1, Pallas kernels, local(): pl.pallas_call(kernel, out_shape=pltpu.VMEM((own, nq), F32), in_specs=[hb...  37 us

profile of v7, /device:TPU:1, one launch (start us, length us, event | category | flops | bytes accessed | tf_op | source)
XLA Modules:
  0.0 37.6 jit_solution(14379566093802101421)
XLA Ops:
  0.0 37.0 %shard_map.73 = f32[16,256]{1,0:T(8,128)S(1)} custom-call(bf16[800,1024]{1,0:T(8,128)(2,1)} %bitcast.4, bf16[160,1024]{1,0:T(8,128)(2,1)} %bitcast.5, bf16[64,800]{1,0:T(8,128)(2,1)} %bitcast.6, bf16[64,160]{1,0:T(8,128)(2,1)} %bitcast.7, bf16[256,4096]{1,0:T(8,128)(2,1)} %qry.1, s32[256]{0:T(256)} %lens.1, s32[256]{0:T(256)} %order.1), custom_call_target="tpu_custom_call" | custom-call | tf_op jit(solution)/shard_map/pallas_call | solution.py:284
  37.0 0.6 %copy.9 = f32[16,256]{1,0:T(8,128)} copy(f32[16,256]{1,0:T(8,128)S(1)} %shard_map.73) | data formatting | bytes 32768
